TPU v7x, 32 devices: a whole 2x2x4 slice. The times are simulated.
32 devices in a mesh: sub: 8 (over z, y), grp: 4 (over x, core).
Axes of the slice: x: 2, y: 2, z: 4, core: 2. Of those that a mesh axis runs over, the one named last changes fastest.
Arguments:
- rhs: float32 [8192, 512], P(('sub', 'grp')), may hold values from -120 to 120
- kappa: float32 [8192], P(('sub', 'grp')), may hold values from 0.5 to 5
- stiffness: float32 [512, 512], replicated, may hold values from -1 to 3
- local_inverse: float32 [512, 512], replicated, may hold values from -1 to 2
- modes: float32 [8, 512], replicated, may hold values from -0.25 to 0.25
- coarse_weight: float32 [8, 8192], P(None, ('sub', 'grp')), may hold values from 0.5 to 1.5
- coarse_mask: int32 [8, 8192], P(None, ('sub', 'grp')), may hold values 0 or 1
- coarse_inverse: float32 [256, 256], P(('sub', 'grp')), may hold values from -1 to 1
- neighbours: int32 [4, 8192], P(None, ('sub', 'grp')), may hold values from -1 to 8191, as said below
Outputs:
- solution: float32 [8192, 512], P(('sub', 'grp'))
Inputs may be any that keep to these rules, and one draw needn't show every extreme that they name: `neighbours`: entries are element numbers or -1. For element e of subdomain d (elements d * 256 to d * 256 + 255), rows 0 and 1 name two other elements of subdomain d, row 2 names an element of subdomain d - 4 or -1, row 3 an element of subdomain d + 4 or -1. Every relation is mutual: row 0 of a names b exactly where row 1 of b names a, and row 3 of a names b exactly where row 2 of b names a. Between subdomains d and d + 4 there are 1 to 64 linked pairs, exactly 64 for some d.
All inputs are finite; a program needn't handle non-finite values. No bound on the sum of `coarse_mask` on one device may be relied on, other than what follows from the above.
Results may differ from a plain program's by a relative error of at most 0.000093.
Values sent between devices are 32-bit elements; how exact they have to be, the bound alone decides.
A program may use at most 64 MiB of HBM per device.

v0:
```python
import jax
import jax.numpy as jnp
from jax import lax
from jax.sharding import PartitionSpec as P

FACE = 64


SIGMA = 1.0
HIGH = lax.Precision.HIGHEST


def padded(block, sides, width):
    for axis, dim in sides:
        count = lax.axis_size(axis)
        forward = [(i, i + 1) for i in range(count - 1)]
        backward = [(target, source) for source, target in forward]
        low = lax.ppermute(
            lax.slice_in_dim(block, block.shape[dim] - width, None, axis=dim), axis, forward
        )
        high = lax.ppermute(lax.slice_in_dim(block, 0, width, axis=dim), axis, backward)
        block = jnp.concatenate([low, block, high], axis=dim)
    return block


def face_values(field):
    width = field.shape[1]
    return jnp.concatenate([field[:, :FACE], field[:, width - FACE :]], axis=1)


def lift_faces(terms, width):
    middle = jnp.zeros((terms.shape[0], width - 2 * FACE), jnp.float32)
    return jnp.concatenate([terms[:, :FACE], middle, terms[:, FACE:]], axis=1)


def body(
    rhs,
    kappa,
    stiffness,
    local_inverse,
    modes,
    coarse_weight,
    coarse_mask,
    coarse_inverse,
    neighbours,
):
    rows, width = rhs.shape
    groups = lax.axis_size("grp")
    device = lax.axis_index("sub") * groups + lax.axis_index("grp")
    valid = neighbours >= 0
    degree = jnp.sum(valid.astype(jnp.float32), axis=0)
    owner = jnp.floor_divide(neighbours, rows)
    side = jnp.floor_divide(owner - device, groups)
    index = jnp.where(valid, (side + 1) * rows + neighbours - owner * rows, 0)

    def operate(field):
        traces = face_values(field)
        window = padded(traces, (("sub", 0),), rows)
        beside = jnp.sum(jnp.where(valid[:, :, None], window[index], 0.0), axis=0)
        penalty = SIGMA * (degree[:, None] * traces - beside)
        return kappa[:, None] * jnp.dot(field, stiffness, precision=HIGH) + lift_faces(
            penalty, width
        )

    weights = coarse_weight * coarse_mask.astype(jnp.float32)

    def add_coarse(piece):
        return jnp.dot(coarse_inverse, piece, precision=HIGH)

    def precondition(residual):
        local_part = jnp.dot(residual, local_inverse, precision=HIGH) / kappa[:, None]
        projected = jnp.einsum("kp,ep->ke", modes, residual, precision=HIGH)
        restricted = jnp.sum(weights * projected, axis=1)
        solved = add_coarse(lax.all_gather(restricted, ("sub", "grp"), axis=0, tiled=True))
        coarse_part = jnp.dot((weights * solved[:, None]).T, modes, precision=HIGH)
        return local_part + coarse_part

    def dots(values):
        return lax.psum(jnp.stack(values), ("sub", "grp"))

    beta = jnp.sqrt(dots([jnp.sum(rhs * rhs)])[0])
    first = rhs / beta
    z_one = precondition(first)
    w_one = operate(z_one)
    sums = dots([jnp.sum(w_one * first), jnp.sum(w_one * w_one)])
    h11 = sums[0]
    s_one = sums[1]
    h21 = jnp.sqrt(s_one - h11 * h11)
    second = (w_one - h11 * first) / h21
    z_two = precondition(second)
    w_two = operate(z_two)
    sums = dots([jnp.sum(w_two * first), jnp.sum(w_two * second), jnp.sum(w_two * w_two)])
    h12 = sums[0]
    h22 = sums[1]
    s_two = sums[2]
    cross = h11 * h12 + h21 * h22
    det = s_one * s_two - cross * cross
    y_one = beta * (h11 * s_two - h12 * cross) / det
    y_two = beta * (h12 * s_one - h11 * cross) / det
    return y_one * z_one + y_two * z_two


def solution(mesh):
    placed = (
        P(("sub", "grp"), None),
        P(("sub", "grp")),
        P(),
        P(),
        P(),
        P(None, ("sub", "grp")),
        P(None, ("sub", "grp")),
        P(("sub", "grp"), None),
        P(None, ("sub", "grp")),
    )
    return jax.shard_map(
        body, mesh=mesh, in_specs=placed, out_specs=P(("sub", "grp"), None), check_vma=False
    )
```

profile of v0, /device:TPU:0, one launch (start us, length us, event | category | flops | bytes accessed | tf_op | source)
XLA Modules:
  0.0 262.0 jit_solution(6855861076460524203)
XLA Ops:
  0.0 1.9 multiply_reduce_fusion.5
  1.9 42.2 %psum.21 = f32[1]{0:T(128)} all-reduce(f32[1]{0:T(128)} %bitcast), channel_id=1, replica_groups=mesh['sub'=8,'grp'=4] {'sub','grp'}, use_global_device_ids=true, to_apply=%region_1.2 | all-reduce | flops 1 | bytes 8 | tf_op jit(solution)/shard_map/psum | solution.py:79
  44.8 0.7 convert_multiply_fusion
  46.4 40.3 %all-reduce = f32[256]{0:T(256)S(1)} all-reduce(f32[256]{0:T(256)S(1)} %dynamic-update-slice), channel_id=1, replica_groups=mesh['sub'=8,'grp'=4] {'sub','grp'}, use_global_device_ids=true, to_apply=%add | all-reduce | flops 256 | bytes 2048
  86.9 0.7 fusion.10
  87.6 1.1 fusion
  88.9 4.2 %collective-permute-start = (f32[256,128]{1,0:T(8,128)S(1)}, f32[256,128]{1,0:T(8,128)S(1)}, u32[]{:S(2)}, u32[]{:S(2)}) collective-permute-start(f32[256,128]{1,0:T(8,128)S(1)} %pad_maximum_fusion.2), channel_id=1, source_target_pairs={{0,4},{4,8},{8,12},{12,16},{16,20},{20,24},{24,28},{1,5},{5,9},{9,... | collective-permute-start | bytes 393224 | tf_op jit(solution)/shard_map/ppermute | solution.py:18
  93.1 1.3 collective-permute-start.1
  94.4 0.7 copy-done.6
  95.2 1.8 collective-permute-done
  97.0 3.0 %collective-permute-done.1 = f32[256,128]{1,0:T(8,128)S(1)} collective-permute-done((f32[256,128]{1,0:T(8,128)S(1)}, f32[256,128]{1,0:T(8,128)S(1)}, u32[]{:S(2)}, u32[]{:S(2)}) %collective-permute-start.1) | collective-permute-done | bytes 131104 | tf_op jit(solution)/shard_map/ppermute | solution.py:21
  100.1 2.8 %gather_fusion = f32[1024,128]{1,0:T(8,128)S(1)} fusion(f32[768,128]{1,0:T(8,128)S(1)} %pad_maximum_fusion, s32[1024]{0:T(1024)S(1)} %broadcast_clamp_fusion), kind=kCustom, calls=%fused_computation | custom fusion | bytes 1052672 | tf_op jit(solution)/shard_map/gather | solution.py:59
  103.3 0.8 copy-done.9
  104.1 1.9 multiply_reduce_fusion.4
  106.0 1.3 pad_maximum_fusion.4
  107.3 40.1 %psum.22 = f32[2]{0:T(128)S(1)} all-reduce(f32[2]{0:T(128)S(1)} %pad_maximum_fusion.4), channel_id=1, replica_groups=mesh['sub'=8,'grp'=4] {'sub','grp'}, use_global_device_ids=true, to_apply=%region_7.8 | all-reduce | flops 2 | bytes 16 | tf_op jit(solution)/shard_map/psum | solution.py:79
  147.3 0.7 fusion.29
  149.8 0.7 subtract_divide_fusion
  151.4 39.0 %all-reduce.1 = f32[256]{0:T(256)S(1)} all-reduce(f32[256]{0:T(256)S(1)} %dynamic-update-slice.1), channel_id=1, replica_groups=mesh['sub'=8,'grp'=4] {'sub','grp'}, use_global_device_ids=true, to_apply=%add.1 | all-reduce | flops 256 | bytes 2048
  190.5 0.7 fusion.8
  191.2 1.1 fusion.2
  192.5 4.2 %collective-permute-start.2 = (f32[256,128]{1,0:T(8,128)S(1)}, f32[256,128]{1,0:T(8,128)S(1)}, u32[]{:S(2)}, u32[]{:S(2)}) collective-permute-start(f32[256,128]{1,0:T(8,128)S(1)} %pad_maximum_fusion.3), channel_id=1, source_target_pairs={{0,4},{4,8},{8,12},{12,16},{16,20},{20,24},{24,28},{1,5},{5,9},{9,... | collective-permute-start | bytes 393224 | tf_op jit(solution)/shard_map/ppermute | solution.py:18
  196.7 1.3 collective-permute-start.3
  198.0 2.6 collective-permute-done.2
  200.6 3.0 %collective-permute-done.3 = f32[256,128]{1,0:T(8,128)S(1)} collective-permute-done((f32[256,128]{1,0:T(8,128)S(1)}, f32[256,128]{1,0:T(8,128)S(1)}, u32[]{:S(2)}, u32[]{:S(2)}) %collective-permute-start.3) | collective-permute-done | bytes 131104 | tf_op jit(solution)/shard_map/ppermute | solution.py:21
  203.7 4.0 %gather_fusion.1 = f32[1024,128]{1,0:T(8,128)} fusion(f32[768,128]{1,0:T(8,128)S(1)} %pad_maximum_fusion.1, s32[1024]{0:T(1024)S(1)} %broadcast_clamp_fusion), kind=kCustom, calls=%fused_computation.1 | custom fusion | bytes 1052672 | tf_op jit(solution)/shard_map/gather | solution.py:59
  207.7 1.3 select_reduce_fusion
  209.3 1.9 multiply_reduce_fusion.2
  211.2 2.0 pad_maximum_fusion.5
  213.1 40.4 %psum.23 = f32[3]{0:T(128)S(1)} all-reduce(f32[3]{0:T(128)S(1)} %pad_maximum_fusion.5), channel_id=1, replica_groups=mesh['sub'=8,'grp'=4] {'sub','grp'}, use_global_device_ids=true, to_apply=%region_13.14 | all-reduce | flops 3 | bytes 24 | tf_op jit(solution)/shard_map/psum | solution.py:79
  253.6 0.7 fusion.28
  261.1 0.9 multiply_add_fusion
  (45 shorter events, 3.4 us)
Async XLA Ops:
  0.0 87.6 %copy-start = (f32[512,512]{1,0:T(8,128)S(1)}, f32[512,512]{1,0:T(8,128)}, u32[]{:S(2)}) copy-start(f32[512,512]{1,0:T(8,128)} %param.12) | copy-start | bytes 3145732
  0.0 45.5 %copy-start.1 = (f32[256,512]{1,0:T(8,128)S(1)}, f32[256,512]{1,0:T(8,128)}, u32[]{:S(2)}) copy-start(f32[256,512]{1,0:T(8,128)} %param.9) | copy-start | bytes 1572868
  1.9 42.9 %copy-start.7 = (f32[8,256]{1,0:T(8,128)S(1)}, f32[8,256]{1,0:T(8,128)}, u32[]{:S(2)}) copy-start(f32[8,256]{1,0:T(8,128)} %param.14) | copy-start | bytes 24580
  44.8 0.7 copy-start.4
  45.5 41.2 %copy-start.5 = (f32[8,256]{1,0:T(8,128)S(1)}, f32[8,256]{1,0:T(8,128)}, u32[]{:S(2)}) copy-start(f32[8,256]{1,0:T(8,128)} %param.16) | copy-start | bytes 24580
  86.9 0.7 copy-start.8
  88.7 14.7 %copy-start.2 = (f32[256,512]{1,0:T(8,128)}, f32[256,512]{1,0:T(8,128)S(1)}, u32[]{:S(2)}) copy-start(f32[256,512]{1,0:T(8,128)S(1)} %fusion) | copy-start | bytes 1572868
  88.9 8.1 %collective-permute-start = (f32[256,128]{1,0:T(8,128)S(1)}, f32[256,128]{1,0:T(8,128)S(1)}, u32[]{:S(2)}, u32[]{:S(2)}) collective-permute-start(f32[256,128]{1,0:T(8,128)S(1)} %pad_maximum_fusion.2), channel_id=1, source_target_pairs={{0,4},{4,8},{8,12},{12,16},{16,20},{20,24},{24,28},{1,5},{5,9},{9,... | collective-permute-start | bytes 393224 | tf_op jit(solution)/shard_map/ppermute | solution.py:18
  93.1 6.9 %collective-permute-start.1 = (f32[256,128]{1,0:T(8,128)S(1)}, f32[256,128]{1,0:T(8,128)S(1)}, u32[]{:S(2)}, u32[]{:S(2)}) collective-permute-start(f32[256,128]{1,0:T(8,128)S(1)} %pad_maximum_fusion.2), channel_id=1, source_target_pairs={{4,0},{8,4},{12,8},{16,12},{20,16},{24,20},{28,24},{5,1},{9,5},{13... | collective-permute-start | bytes 393224 | tf_op jit(solution)/shard_map/ppermute | solution.py:21
  94.4 0.7 copy-start.6
  102.9 1.2 copy-start.9
  192.5 8.1 %collective-permute-start.2 = (f32[256,128]{1,0:T(8,128)S(1)}, f32[256,128]{1,0:T(8,128)S(1)}, u32[]{:S(2)}, u32[]{:S(2)}) collective-permute-start(f32[256,128]{1,0:T(8,128)S(1)} %pad_maximum_fusion.3), channel_id=1, source_target_pairs={{0,4},{4,8},{8,12},{12,16},{16,20},{20,24},{24,28},{1,5},{5,9},{9,... | collective-permute-start | bytes 393224 | tf_op jit(solution)/shard_map/ppermute | solution.py:18
  196.7 6.9 %collective-permute-start.3 = (f32[256,128]{1,0:T(8,128)S(1)}, f32[256,128]{1,0:T(8,128)S(1)}, u32[]{:S(2)}, u32[]{:S(2)}) collective-permute-start(f32[256,128]{1,0:T(8,128)S(1)} %pad_maximum_fusion.3), channel_id=1, source_target_pairs={{4,0},{8,4},{12,8},{16,12},{20,16},{24,20},{28,24},{5,1},{9,5},{13... | collective-permute-start | bytes 393224 | tf_op jit(solution)/shard_map/ppermute | solution.py:21
  207.7 1.6 copy-start.10
  209.3 51.9 %copy-start.3 = (f32[256,512]{1,0:T(8,128)S(1)}, f32[256,512]{1,0:T(8,128)}, u32[]{:S(2)}) copy-start(f32[256,512]{1,0:T(8,128)} %copy-done.2) | copy-start | bytes 1572868
where the time goes:
time: 263 us; the launch traced here: 262 us
  blocking collectives  202 us (77%)
  starting transfers between devices  10.9 us (4%)
  local copies, waits for them, and re-layouts  10.6 us (4%)
  waiting for transfers between devices  10.3 us (4%)
  other arithmetic  9.72 us (4%)
  between operations  9.72 us (4%)
  matrix products  8.79 us (3%)
    psum x3, blocking collectives, dots(): return lax.psum(jnp.stack(values), ('sub', 'grp'))  123 us
    unnamed x2, blocking collectives  79.3 us
    ppermute x2, starting transfers between devices, padded(): lax.ppermute(lax.slice_in_dim(block, block.shape[dim] - width, None, axis...  8.36 us
    gather x2, local copies, waits for them, and re-layouts, operate(): beside = jnp.sum(jnp.where(valid[:, :, None], window[index], 0.0), axis=0)  6.81 us
    ppermute x2, waiting for transfers between devices, padded(): lax.ppermute(lax.slice_in_dim(block, 0, width, axis=dim), axis, backward)  5.93 us
  transfers between devices with their start and end apart: 4, of which 4 were waited for; matrix products, arithmetic and copies ran while one was open for 0% of the time, Pallas kernels for 0%

commit v1 on v0

v1 whole, which is shorter than its diff:
```python
import functools

import jax
import jax.numpy as jnp
from jax import lax
from jax.experimental import pallas as pl
from jax.experimental.pallas import tpu as pltpu
from jax.sharding import PartitionSpec as P

FACE = 64
BND = 64
SIGMA = 1.0
LANES = 128
HALF = 64
MESH = pl.DeviceIdType.MESH
F32 = jnp.float32
BF16 = jnp.bfloat16


def parts(x):
    high = x.astype(BF16).astype(F32)
    return high, x - high


def dot(a, b):
    return jnp.dot(a, b, preferred_element_type=F32)


def dot_t(a, b):
    return lax.dot_general(a, b, (((1,), (1,)), ((), ())), preferred_element_type=F32)


def iota(shape, dim):
    return lax.broadcasted_iota(jnp.int32, shape, dim)


def total(x):
    return jnp.sum(jnp.sum(x, axis=0, keepdims=True), axis=1, keepdims=True)


def kernel(
    subs, groups,
    rhs_h, kappa_h, st_h, li_h, modes_h, cw_h, cm_h, ci_h, nb_h,
    out_ref,
    rhs, kappa, st, li, modes, cw, cm, nb, cx,
    msg, gbuf, hs, hbuf,
    xh, xl, lh, ll, sh, sl, p_one, p_two, acc, w_one, z_one, pen,
    lsem, gsend, grecv, hsend, hrecv, csend, crecv,
):
    n = subs * groups
    sub = lax.axis_index("sub")
    grp = lax.axis_index("grp")
    me = sub * groups + grp
    rows, width = rhs.shape
    coarse = modes.shape[0]
    nc = ci_h.shape[1]
    last = width - LANES

    loads = [
        pltpu.make_async_copy(src, dst, lsem.at[i])
        for i, (src, dst) in enumerate(
            [
                (rhs_h, rhs), (cw_h, cw), (cm_h, cm), (modes_h, modes), (li_h, li),
                (nb_h, nb), (kappa_h, kappa), (ci_h, cx.at[0, :, pl.ds(0, nc)]), (st_h, st),
            ]
        )
    ]
    for load in loads:
        load.start()

    barrier = pltpu.get_barrier_semaphore()

    def greet(i, carry):
        t = lax.rem(me + i, n)
        pl.semaphore_signal(
            barrier, inc=1, device_id=(t // groups, lax.rem(t, groups)), device_id_type=MESH
        )
        return carry

    lax.fori_loop(1, n, greet, 0)

    def share(step):
        def one(i, carry):
            t = lax.rem(me + i, n)
            pltpu.make_async_remote_copy(
                src_ref=msg.at[step],
                dst_ref=gbuf.at[step, me],
                send_sem=gsend.at[step],
                recv_sem=grecv.at[step],
                device_id=(t // groups, lax.rem(t, groups)),
                device_id_type=MESH,
            ).start()
            return carry

        lax.fori_loop(1, n, one, 0)
        gbuf[step, me] = msg[step]

    def await_all(step, sem):
        pltpu.make_async_copy(
            gbuf.at[step, pl.ds(0, n - 1)], gbuf.at[step, pl.ds(0, n - 1)], sem.at[step]
        ).wait()

    lane = iota((1, LANES), 1)
    place = lax.rem(me, 16) * coarse
    aside = HALF - HALF * lax.rem(me // 8, 2)

    def fill(step, column, scalars):
        line = jnp.zeros((1, LANES), F32)
        if column is not None:
            spot = iota((coarse, LANES), 1) == iota((coarse, LANES), 0) + place
            line = jnp.sum(jnp.where(spot, column, 0.0), axis=0, keepdims=True)
        for i, value in enumerate(scalars):
            line = line + jnp.where(lane == aside + i, value, 0.0)
        msg[step] = line

    def collect(step):
        chunks = []
        sums = jnp.zeros((1, LANES), F32)
        for c in range(n // 16):
            even = jnp.sum(gbuf[step, pl.ds(16 * c, 8)], axis=0)
            odd = jnp.sum(gbuf[step, pl.ds(16 * c + 8, 8)], axis=0)
            chunks.append(jnp.where(lane < HALF, even, odd))
            sums = sums + jnp.where(lane < HALF, odd, even)
        return chunks, sums

    def scalar(sums, i):
        return jnp.sum(
            jnp.where((lane == i) | (lane == HALF + i), sums, 0.0), axis=1, keepdims=True
        )

    for i in (0, 1, 2, 3):
        loads[i].wait()
    weights = cw[...] * cm[...].astype(F32)
    w_high, w_low = parts(weights)
    w_stack = jnp.concatenate([w_high, w_low], axis=0).astype(BF16)

    def split_to(value, high_ref, low_ref):
        high = value.astype(BF16)
        high_ref[...] = high
        low_ref[...] = (value - high.astype(F32)).astype(BF16)

    def restrict():
        both = dot(w_stack, xh[...]) + dot(w_stack, xl[...])
        return jnp.sum(
            (both[:coarse] + both[coarse:]) * modes[...], axis=1, keepdims=True
        )

    split_to(rhs[...], xh, xl)
    fill(0, restrict(), [total(rhs[...] * rhs[...])])
    pl.semaphore_wait(barrier, n - 1)
    share(0)

    up = (lax.rem(sub + 1, subs), grp)
    down = (lax.rem(sub + subs - 1, subs), grp)

    loads[5].wait()
    loads[6].wait()
    base = me * rows
    square = (rows, rows)
    across, along = iota(square, 0), iota(square, 1)
    near = jnp.where(across == nb[0:1, :] - base, 1.0, 0.0) + jnp.where(
        across == nb[1:2, :] - base, 1.0, 0.0
    )
    near = near.astype(BF16)
    below, above = nb[2:3, :].astype(F32), nb[3:4, :].astype(F32)
    degree = jnp.sum(jnp.where(nb[...] >= 0, 1.0, 0.0), axis=0, keepdims=True)
    pad = jnp.zeros((4, rows), F32)
    columns = jnp.concatenate([below, above, kappa[...], degree, pad], axis=0).T
    below_c, above_c = columns[:, 0:1], columns[:, 1:2]
    kappa_c, degree_c = columns[:, 2:3], columns[:, 3:4]
    inverse_c = 1.0 / kappa_c

    def packing(line, column):
        rank = jnp.sum(
            jnp.where((column >= 0.0) & (column < line), 1.0, 0.0), axis=0, keepdims=True
        )
        hit = (iota((BND, rows), 0).astype(F32) == rank) & (line >= 0.0)
        return jnp.where(hit, 1.0, 0.0)

    pack = jnp.concatenate([packing(above, above_c), packing(below, below_c)], axis=0).astype(BF16)
    packed = dot_t(w_stack, pack)
    cx[0, :, pl.ds(nc, LANES)] = packed[:coarse] + packed[coarse:]
    loads[7].wait()

    def coarse_copy(way, target):
        return pltpu.make_async_remote_copy(
            src_ref=cx.at[0], dst_ref=cx.at[1 + way],
            send_sem=csend.at[way], recv_sem=crecv.at[way],
            device_id=target, device_id_type=MESH,
        )

    coarse_copies = [coarse_copy(0, up), coarse_copy(1, down)]
    for copy in coarse_copies:
        copy.start()

    def rank_of(line):
        return jnp.sum(
            jnp.where((line >= 0.0) & (along < across), 1.0, 0.0), axis=1, keepdims=True
        )

    rank_below, rank_above = rank_of(below), rank_of(above)
    wide = (rows, LANES)
    lane_f = iota(wide, 1).astype(F32)
    first_half = lane_f < HALF
    put = jnp.where(
        first_half,
        jnp.where((below_c >= 0.0) & (lane_f == rank_below), 1.0, 0.0),
        jnp.where((above_c >= 0.0) & (lane_f - HALF == rank_above), 1.0, 0.0),
    ).astype(BF16)

    loads[4].wait()
    split_to(li[...], lh, ll)

    def product(high, low, m_high, m_low):
        return dot(high[...], m_high[...]) + dot(high[...], m_low[...]) + dot(low[...], m_high[...])

    def beside(matrix, value):
        high, low = parts(value)
        both = dot(matrix, jnp.concatenate([high, low], axis=1).astype(BF16))
        return both[:, :LANES] + both[:, LANES:]

    def halo_copy(step, way, target):
        block = pl.ds(BND * way, BND)
        return pltpu.make_async_remote_copy(
            src_ref=hs.at[step, block, :], dst_ref=hbuf.at[step, block, :],
            send_sem=hsend.at[step, way], recv_sem=hrecv.at[step, way],
            device_id=target, device_id_type=MESH,
        )

    def traces_of(ref):
        return jnp.where(first_half, ref[:, 0:LANES], ref[:, last:width])

    def start_local(step, ref):
        ref[...] = product(xh, xl, lh, ll) * inverse_c
        traces = traces_of(ref)
        hs[step] = beside(pack, traces)
        copies = [halo_copy(step, 0, up), halo_copy(step, 1, down)]
        for copy in copies:
            copy.start()
        return copies

    def finish_local(step, ref, copies):
        traces = traces_of(ref)
        pen[...] = degree_c * traces - beside(near, traces)
        split_to(ref[...], xh, xl)
        acc[...] = product(xh, xl, sh, sl) * kappa_c
        for copy in copies:
            copy.wait_recv()
        lifted = SIGMA * (pen[...] - beside(put, hbuf[step]))
        acc[:, 0:LANES] += jnp.where(first_half, lifted, 0.0)
        acc[:, last:width] += jnp.where(first_half, 0.0, lifted)

    halo_one = start_local(0, p_one)

    loads[8].wait()
    split_to(st[...], sh, sl)

    m_high, m_low = parts(modes[...])
    m_stack = jnp.concatenate([m_high, m_low], axis=0).astype(BF16)
    ms = dot(m_stack, sh[...]) + dot(m_stack, sl[...])
    ms = ms[:coarse] + ms[coarse:]
    column = iota((coarse, width), 1)
    faces = SIGMA * jnp.where((column < FACE) | (column >= width - FACE), modes[...], 0.0)
    linked = dot(w_stack, near)
    linked = linked[:coarse] + linked[coarse:]
    finish_local(0, p_one, halo_one)

    for copy in coarse_copies:
        copy.wait_recv()
    lane_w = iota((coarse, LANES), 1)
    from_below = jnp.where(lane_w < HALF, cx[1, :, pl.ds(nc, LANES)], 0.0)
    from_above = jnp.where(lane_w < HALF, 0.0, cx[2, :, pl.ds(nc, LANES)])
    lows, highs = parts(from_below), parts(from_above)
    outer = dot_t(
        jnp.concatenate([lows[0], highs[0], lows[1], highs[1]], axis=0).astype(BF16), put
    )
    outer = outer[: 2 * coarse] + outer[2 * coarse :]
    k_high, k_low = parts(
        jnp.concatenate([kappa[...] * weights, degree * weights - linked, -outer], axis=0)
    )
    mix = jnp.concatenate([k_high, k_low, k_high], axis=0).T.astype(BF16)
    spread = jnp.concatenate(
        [w_high, w_low, w_high, jnp.zeros_like(w_high)], axis=0
    ).T.astype(BF16)

    def stacked(value):
        high, low = parts(value)
        return [high, high, low]

    def solve(chunks):
        whole = jnp.concatenate(chunks, axis=1)
        return jnp.sum(cx[:, :, pl.ds(0, nc)] * whole[None], axis=2, keepdims=True)

    def add_to_w(y):
        own = y[0]
        values = jnp.concatenate(
            [ms * own, faces * own, faces * y[1], faces * y[2]], axis=0
        )
        return dot(mix, jnp.concatenate(stacked(values), axis=0).astype(BF16))

    def add_to_z(y):
        values = stacked(modes[...] * y[0])
        return dot(
            spread, jnp.concatenate(values + [jnp.zeros_like(values[0])], axis=0).astype(BF16)
        )

    await_all(0, grecv)
    chunks, sums = collect(0)
    beta = jnp.sqrt(scalar(sums, 0))
    scale = 1.0 / beta
    y = solve(chunks) * scale[None]
    w_one[...] = acc[...] * scale + add_to_w(y)
    split_to(w_one[...], xh, xl)
    fill(
        1,
        restrict(),
        [total(w_one[...] * rhs[...]) * scale, total(w_one[...] * w_one[...])],
    )
    share(1)

    halo_two = start_local(1, p_two)
    finish_local(1, p_two, halo_two)
    z_one[...] = p_one[...] * scale + add_to_z(y)

    await_all(1, grecv)
    chunks, sums = collect(1)
    h11 = scalar(sums, 0)
    s_one = scalar(sums, 1)
    h21 = jnp.sqrt(s_one - h11 * h11)
    over = 1.0 / h21
    y = solve(chunks)
    acc[...] = (acc[...] + add_to_w(y) - h11 * w_one[...]) * over
    first = total(acc[...] * rhs[...]) * scale
    second = total(acc[...] * (w_one[...] - (h11 * scale) * rhs[...])) * over
    third = total(acc[...] * acc[...])
    fill(2, None, [first, second, third])
    share(2)
    p_two[...] = (p_two[...] + add_to_z(y) - h11 * z_one[...]) * over

    await_all(2, grecv)
    chunks, sums = collect(2)
    h12, h22, s_two = scalar(sums, 0), scalar(sums, 1), scalar(sums, 2)
    cross = h11 * h12 + h21 * h22
    det = s_one * s_two - cross * cross
    y_one = beta * (h11 * s_two - h12 * cross) / det
    y_two = beta * (h12 * s_one - h11 * cross) / det
    out_ref[...] = y_one * z_one[...] + y_two * p_two[...]

    for step in range(3):
        await_all(step, gsend)
    for copy in coarse_copies + halo_one + halo_two:
        copy.wait_send()


def body(subs, groups, rhs, kappa, stiffness, local_inverse, modes, cw, cm, ci, nb):
    rows, width = rhs.shape
    n = subs * groups
    coarse, nc = ci.shape
    square = (width, width)
    vmem = pltpu.VMEM
    dma = pltpu.SemaphoreType.DMA
    return pl.pallas_call(
        functools.partial(kernel, subs, groups),
        out_shape=jax.ShapeDtypeStruct((rows, width), F32),
        in_specs=[pl.BlockSpec(memory_space=pl.ANY)] * 9,
        out_specs=pl.BlockSpec(memory_space=pltpu.VMEM),
        scratch_shapes=[
            vmem((rows, width), F32), vmem((1, rows), F32), vmem(square, F32), vmem(square, F32),
            vmem((coarse, width), F32), vmem((coarse, rows), F32), vmem((coarse, rows), jnp.int32),
            vmem((4, rows), jnp.int32), vmem((3, coarse, nc + LANES), F32),
            vmem((3, 1, LANES), F32), vmem((3, n, 1, LANES), F32),
            vmem((2, 2 * BND, LANES), F32), vmem((2, 2 * BND, LANES), F32),
            vmem((rows, width), BF16), vmem((rows, width), BF16),
            vmem(square, BF16), vmem(square, BF16), vmem(square, BF16), vmem(square, BF16),
            vmem((rows, width), F32), vmem((rows, width), F32), vmem((rows, width), F32),
            vmem((rows, width), F32), vmem((rows, width), F32), vmem((rows, LANES), F32),
            dma((9,)), dma((3,)), dma((3,)), dma((2, 2)), dma((2, 2)), dma((2,)), dma((2,)),
        ],
        compiler_params=pltpu.CompilerParams(
            collective_id=0, has_side_effects=True, vmem_limit_bytes=48 * 1024 * 1024
        ),
    )(rhs, kappa.reshape(1, rows), stiffness, local_inverse, modes, cw, cm, ci, nb)


def solution(mesh):
    placed = (
        P(("sub", "grp"), None),
        P(("sub", "grp")),
        P(),
        P(),
        P(),
        P(None, ("sub", "grp")),
        P(None, ("sub", "grp")),
        P(("sub", "grp"), None),
        P(None, ("sub", "grp")),
    )
    return jax.shard_map(
        functools.partial(body, mesh.shape["sub"], mesh.shape["grp"]),
        mesh=mesh, in_specs=placed, out_specs=P(("sub", "grp"), None), check_vma=False,
    )
```

time: 263 us -> 32.8 us (0.12)
  blocking collectives: 202 us -> 0 us
  Pallas kernels: 0 us -> 23.9 us
  starting transfers between devices: 10.9 us -> 0 us
  waiting for transfers between devices: 10.3 us -> 0 us
  other arithmetic: 9.72 us -> 0 us
  between operations: 9.72 us -> 0.02 us
  matrix products: 8.79 us -> 0 us
    psum x3 -> x0, blocking collectives: 123 us -> none  [dots(): return lax.psum(jnp.stack(values), ('sub', 'grp'))]
    unnamed x2 -> x0, blocking collectives: 79.3 us -> none
    pallas_call x0 -> x1, Pallas kernels: none -> 23.9 us  [body(): pl.pallas_call(functools.partial(kernel, subs, groups), out_shape=jax.Sha...]
    ppermute x4 -> x0, starting transfers between devices: 10.9 us -> none  [the longest x2 8.36 us: padded(): lax.ppermute(lax.slice_in_dim(block, block.shape[dim] - width, None, axis...]
    ppermute x4 -> x0, waiting for transfers between devices: 10.3 us -> none  [the longest x2 5.93 us: padded(): lax.ppermute(lax.slice_in_dim(block, 0, width, axis=dim), axis, backward)]
    dot_general x10 -> x0, matrix products: 8.79 us -> none  [the longest x2 3.75 us: operate(): jnp.dot(field, stiffness, precision=HIGH)]
    gather x2 -> x0, local copies, waits for them, and re-layouts: 6.81 us -> none  [operate(): beside = jnp.sum(jnp.where(valid[:, :, None], window[index], 0.0), axis=0)]
    unnamed x27 -> x19, local copies, waits for them, and re-layouts: 1.97 us -> 8.46 us
  transfers between devices with their start and end apart: 4 -> 0, of which waited for: 4 -> 0; matrix products, arithmetic and copies ran while one was open for 0% -> 0% of each run, Pallas kernels for 0% -> 0%
where the time goes in v1:
time: 32.8 us; the launch traced here: 32.4 us
  Pallas kernels  23.9 us (73%)
  local copies, waits for them, and re-layouts  8.46 us (26%)
    pallas_call x1, Pallas kernels, body(): pl.pallas_call(functools.partial(kernel, subs, groups), out_shape=jax.Sha...  23.9 us
    unnamed x19, local copies, waits for them, and re-layouts  8.46 us

profile of v1, /device:TPU:0, one launch (start us, length us, event | category | flops | bytes accessed | tf_op | source)
XLA Modules:
  0.0 32.4 jit_solution(16938194947718867412)
XLA Ops:
  0.0 0.0 copy-start.8
  0.0 0.7 %copy-done.8 = f32[256]{0:T(256)S(1)} copy-done((f32[256]{0:T(256)S(1)}, f32[256]{0:T(256)}, u32[]{:S(2)}) %copy-start.8) | copy-done | bytes 1048
  0.7 0.0 copy-start
  0.7 1.2 %copy-done = f32[512,512]{1,0:T(8,128)S(1)} copy-done((f32[512,512]{1,0:T(8,128)S(1)}, f32[512,512]{1,0:T(8,128)}, u32[]{:S(2)}) %copy-start) | copy-done | bytes 1048600
  1.9 0.0 copy-start.1
  1.9 1.2 %copy-done.1 = f32[512,512]{1,0:T(8,128)S(1)} copy-done((f32[512,512]{1,0:T(8,128)S(1)}, f32[512,512]{1,0:T(8,128)}, u32[]{:S(2)}) %copy-start.1) | copy-done | bytes 1048600
  3.1 0.0 copy-start.2
  3.1 1.0 %copy-done.2 = f32[256,512]{1,0:T(8,128)S(1)} copy-done((f32[256,512]{1,0:T(8,128)S(1)}, f32[256,512]{1,0:T(8,128)}, u32[]{:S(2)}) %copy-start.2) | copy-done | bytes 524312
  4.2 0.0 copy-start.3
  4.2 0.7 %copy-done.3 = f32[8,512]{1,0:T(8,128)S(1)} copy-done((f32[8,512]{1,0:T(8,128)S(1)}, f32[8,512]{1,0:T(8,128)}, u32[]{:S(2)}) %copy-start.3) | copy-done | bytes 16408
  4.9 0.0 copy-start.4
  4.9 0.7 %copy-done.4 = f32[8,256]{1,0:T(8,128)S(1)} copy-done((f32[8,256]{1,0:T(8,128)S(1)}, f32[8,256]{1,0:T(8,128)}, u32[]{:S(2)}) %copy-start.4) | copy-done | bytes 8216
  5.6 0.0 copy-start.5
  5.6 0.7 %copy-done.5 = s32[8,256]{1,0:T(8,128)S(1)} copy-done((s32[8,256]{1,0:T(8,128)S(1)}, s32[8,256]{1,0:T(8,128)}, u32[]{:S(2)}) %copy-start.5) | copy-done | bytes 8216
  6.3 0.0 copy-start.6
  6.3 0.7 %copy-done.6 = f32[8,256]{1,0:T(8,128)S(1)} copy-done((f32[8,256]{1,0:T(8,128)S(1)}, f32[8,256]{1,0:T(8,128)}, u32[]{:S(2)}) %copy-start.6) | copy-done | bytes 8216
  7.0 0.0 copy-start.7
  7.0 0.7 %copy-done.7 = s32[4,256]{1,0:T(4,128)S(1)} copy-done((s32[4,256]{1,0:T(4,128)S(1)}, s32[4,256]{1,0:T(4,128)}, u32[]{:S(2)}) %copy-start.7) | copy-done | bytes 4120
  7.7 23.9 %shard_map.91 = f32[256,512]{1,0:T(8,128)S(1)} custom-call(f32[256,512]{1,0:T(8,128)S(1)} %copy-done.2, f32[1,256]{1,0:T(1,128)S(1)} %bitcast.1, f32[512,512]{1,0:T(8,128)S(1)} %copy-done, f32[512,512]{1,0:T(8,128)S(1)} %copy-done.1, f32[8,512]{1,0:T(8,128)S(1)} %copy-done.3, f32[8,256]{1,0:T(8,128)S(1)} %copy-done.4, s32[8,256]{1,0:T(8,128)S(1)} %copy-done.5, ...), custom_call_target="tpu_custom_call" | custom-call | tf_op jit(solution)/shard_map/pallas_call | solution.py:362
  31.6 0.8 %copy.11 = f32[256,512]{1,0:T(8,128)} copy(f32[256,512]{1,0:T(8,128)S(1)} %shard_map.91) | data formatting | bytes 1048576
Async XLA Ops:
  0.0 0.7 %copy-start.8 = (f32[256]{0:T(256)S(1)}, f32[256]{0:T(256)}, u32[]{:S(2)}) copy-start(f32[256]{0:T(256)} %param.10) | copy-start | bytes 3076
  0.7 1.2 %copy-start = (f32[512,512]{1,0:T(8,128)S(1)}, f32[512,512]{1,0:T(8,128)}, u32[]{:S(2)}) copy-start(f32[512,512]{1,0:T(8,128)} %st_h.1) | copy-start | bytes 3145732
  1.9 1.2 %copy-start.1 = (f32[512,512]{1,0:T(8,128)S(1)}, f32[512,512]{1,0:T(8,128)}, u32[]{:S(2)}) copy-start(f32[512,512]{1,0:T(8,128)} %li_h.1) | copy-start | bytes 3145732
  3.1 1.0 %copy-start.2 = (f32[256,512]{1,0:T(8,128)S(1)}, f32[256,512]{1,0:T(8,128)}, u32[]{:S(2)}) copy-start(f32[256,512]{1,0:T(8,128)} %rhs_h.1) | copy-start | bytes 1572868
  4.2 0.7 %copy-start.3 = (f32[8,512]{1,0:T(8,128)S(1)}, f32[8,512]{1,0:T(8,128)}, u32[]{:S(2)}) copy-start(f32[8,512]{1,0:T(8,128)} %modes_h.1) | copy-start | bytes 49156
  4.9 0.7 %copy-start.4 = (f32[8,256]{1,0:T(8,128)S(1)}, f32[8,256]{1,0:T(8,128)}, u32[]{:S(2)}) copy-start(f32[8,256]{1,0:T(8,128)} %cw_h.1) | copy-start | bytes 24580
  5.6 0.7 %copy-start.5 = (s32[8,256]{1,0:T(8,128)S(1)}, s32[8,256]{1,0:T(8,128)}, u32[]{:S(2)}) copy-start(s32[8,256]{1,0:T(8,128)} %cm_h.1) | copy-start | bytes 24580
  6.3 0.7 %copy-start.6 = (f32[8,256]{1,0:T(8,128)S(1)}, f32[8,256]{1,0:T(8,128)}, u32[]{:S(2)}) copy-start(f32[8,256]{1,0:T(8,128)} %ci_h.1) | copy-start | bytes 24580
  7.0 0.7 %copy-start.7 = (s32[4,256]{1,0:T(4,128)S(1)}, s32[4,256]{1,0:T(4,128)}, u32[]{:S(2)}) copy-start(s32[4,256]{1,0:T(4,128)} %nb_h.1) | copy-start | bytes 12292

commit v2 on v1

--- a/solution.py
+++ b/solution.py
@@ -362,7 +362,7 @@
     return pl.pallas_call(
         functools.partial(kernel, subs, groups),
         out_shape=jax.ShapeDtypeStruct((rows, width), F32),
-        in_specs=[pl.BlockSpec(memory_space=pl.ANY)] * 9,
+        in_specs=[pl.BlockSpec(memory_space=pltpu.HBM)] * 9,
         out_specs=pl.BlockSpec(memory_space=pltpu.VMEM),
         scratch_shapes=[
             vmem((rows, width), F32), vmem((1, rows), F32), vmem(square, F32), vmem(square, F32),
@@ -377,7 +377,7 @@
             dma((9,)), dma((3,)), dma((3,)), dma((2, 2)), dma((2, 2)), dma((2,)), dma((2,)),
         ],
         compiler_params=pltpu.CompilerParams(
-            collective_id=0, has_side_effects=True, vmem_limit_bytes=48 * 1024 * 1024
+            collective_id=0, has_side_effects=True, vmem_limit_bytes=int(62 * 1024 * 1024)
         ),
     )(rhs, kappa.reshape(1, rows), stiffness, local_inverse, modes, cw, cm, ci, nb)
 

time: 32.8 us -> 26.7 us (0.81)
  local copies, waits for them, and re-layouts: 8.46 us -> 1.87 us
  Pallas kernels: 23.9 us -> 24.7 us
    unnamed x19 -> x1, local copies, waits for them, and re-layouts: 8.46 us -> 1.87 us
    pallas_call x1, Pallas kernels: 23.9 us -> 24.7 us  [body(): pl.pallas_call(functools.partial(kernel, subs, groups), out_shape=jax.Sha...]
where the time goes in v2:
time: 26.7 us; the launch traced here: 26.5 us
  Pallas kernels  24.7 us (93%)
  local copies, waits for them, and re-layouts  1.87 us (7%)
    pallas_call x1, Pallas kernels, body(): pl.pallas_call(functools.partial(kernel, subs, groups), out_shape=jax.Sha...  24.7 us
    unnamed x1, local copies, waits for them, and re-layouts  1.87 us

profile of v2, /device:TPU:0, one launch (start us, length us, event | category | flops | bytes accessed | tf_op | source)
XLA Modules:
  0.0 26.5 jit_solution(4877884148637214523)
XLA Ops:
  0.0 24.7 %shard_map.91 = f32[256,512]{1,0:T(8,128)} custom-call(f32[256,512]{1,0:T(8,128)} %rhs_h.1, f32[1,256]{1,0:T(1,128)} %bitcast.1, f32[512,512]{1,0:T(8,128)} %st_h.1, f32[512,512]{1,0:T(8,128)} %li_h.1, f32[8,512]{1,0:T(8,128)} %modes_h.1, f32[8,256]{1,0:T(8,128)} %cw_h.1, s32[8,256]{1,0:T(8,128)} %cm_h.1, f32[8,256]{1,0:T(8,128)} %ci_h.1, s32[4,256]{1,0:T(4,128)} %nb_h.1), custom_call_target="tpu_custom_call" | custom-call | tf_op jit(solution)/shard_map/pallas_call | solution.py:362
  24.7 1.9 %copy.11 = f32[256,512]{1,0:T(8,128)} copy(f32[256,512]{1,0:T(8,128)} %shard_map.91) | data formatting | bytes 1048576

commit v3 on v2

--- a/solution.py
+++ b/solution.py
@@ -70,29 +70,51 @@
 
     barrier = pltpu.get_barrier_semaphore()
 
-    def greet(i, carry):
-        t = lax.rem(me + i, n)
-        pl.semaphore_signal(
-            barrier, inc=1, device_id=(t // groups, lax.rem(t, groups)), device_id_type=MESH
-        )
-        return carry
-
-    lax.fori_loop(1, n, greet, 0)
+    peers = [lax.rem(grp + j, groups) for j in range(groups)]
+
+    def each_other(act):
+        def plane(i, carry):
+            other = lax.rem(sub + i, subs)
+            for peer in peers:
+                act((other, peer))
+            return carry
+
+        if subs <= 8:
+            for i in sorted(range(1, subs), key=lambda i: abs(i - subs // 2)):
+                plane(i, 0)
+        else:
+            lax.fori_loop(1, subs, plane, 0)
+        for peer in peers[1:]:
+            act((sub, peer))
+
+    each_other(
+        lambda target: pl.semaphore_signal(
+            barrier, inc=1, device_id=target, device_id_type=MESH
+        )
+    )
+    has_up, has_down = sub < subs - 1, sub > 0
+
+    @pl.when(sub == 0)
+    def _():
+        hbuf[:, 0:BND, :] = jnp.zeros((2, BND, LANES), F32)
+        cx[1] = jnp.zeros(cx.shape[1:], F32)
+
+    @pl.when(sub == subs - 1)
+    def _():
+        hbuf[:, BND:, :] = jnp.zeros((2, BND, LANES), F32)
+        cx[2] = jnp.zeros(cx.shape[1:], F32)
 
     def share(step):
-        def one(i, carry):
-            t = lax.rem(me + i, n)
-            pltpu.make_async_remote_copy(
+        each_other(
+            lambda target: pltpu.make_async_remote_copy(
                 src_ref=msg.at[step],
                 dst_ref=gbuf.at[step, me],
                 send_sem=gsend.at[step],
                 recv_sem=grecv.at[step],
-                device_id=(t // groups, lax.rem(t, groups)),
+                device_id=target,
                 device_id_type=MESH,
             ).start()
-            return carry
-
-        lax.fori_loop(1, n, one, 0)
+        )
         gbuf[step, me] = msg[step]
 
     def await_all(step, sem):
@@ -189,9 +211,20 @@
             device_id=target, device_id_type=MESH,
         )
 
+    def start(copies):
+        pl.when(has_up)(copies[0].start)
+        pl.when(has_down)(copies[1].start)
+
+    def arrive(copies):
+        pl.when(has_down)(copies[0].wait_recv)
+        pl.when(has_up)(copies[1].wait_recv)
+
+    def leave(copies):
+        pl.when(has_up)(copies[0].wait_send)
+        pl.when(has_down)(copies[1].wait_send)
+
     coarse_copies = [coarse_copy(0, up), coarse_copy(1, down)]
-    for copy in coarse_copies:
-        copy.start()
+    start(coarse_copies)
 
     def rank_of(line):
         return jnp.sum(
@@ -235,8 +268,7 @@
         traces = traces_of(ref)
         hs[step] = beside(pack, traces)
         copies = [halo_copy(step, 0, up), halo_copy(step, 1, down)]
-        for copy in copies:
-            copy.start()
+        start(copies)
         return copies
 
     def finish_local(step, ref, copies):
@@ -244,8 +276,7 @@
         pen[...] = degree_c * traces - beside(near, traces)
         split_to(ref[...], xh, xl)
         acc[...] = product(xh, xl, sh, sl) * kappa_c
-        for copy in copies:
-            copy.wait_recv()
+        arrive(copies)
         lifted = SIGMA * (pen[...] - beside(put, hbuf[step]))
         acc[:, 0:LANES] += jnp.where(first_half, lifted, 0.0)
         acc[:, last:width] += jnp.where(first_half, 0.0, lifted)
@@ -265,8 +296,7 @@
     linked = linked[:coarse] + linked[coarse:]
     finish_local(0, p_one, halo_one)
 
-    for copy in coarse_copies:
-        copy.wait_recv()
+    arrive(coarse_copies)
     lane_w = iota((coarse, LANES), 1)
     from_below = jnp.where(lane_w < HALF, cx[1, :, pl.ds(nc, LANES)], 0.0)
     from_above = jnp.where(lane_w < HALF, 0.0, cx[2, :, pl.ds(nc, LANES)])
@@ -348,8 +378,8 @@
 
     for step in range(3):
         await_all(step, gsend)
-    for copy in coarse_copies + halo_one + halo_two:
-        copy.wait_send()
+    for copies in (coarse_copies, halo_one, halo_two):
+        leave(copies)
 
 
 def body(subs, groups, rhs, kappa, stiffness, local_inverse, modes, cw, cm, ci, nb):

time: 26.7 us -> 25.5 us (0.955)
  Pallas kernels: 24.7 us -> 23.4 us
    pallas_call x1, Pallas kernels: 24.7 us -> 23.4 us  [body(): pl.pallas_call(functools.partial(kernel, subs, groups), out_shape=jax.Sha...]
where the time goes in v3:
time: 25.5 us; the launch traced here: 25.3 us
  Pallas kernels  23.4 us (92%)
  local copies, waits for them, and re-layouts  1.87 us (7%)
    pallas_call x1, Pallas kernels, body(): pl.pallas_call(functools.partial(kernel, subs, groups), out_shape=jax.Sha...  23.4 us
    unnamed x1, local copies, waits for them, and re-layouts  1.87 us

profile of v3, /device:TPU:0, one launch (start us, length us, event | category | flops | bytes accessed | tf_op | source)
XLA Modules:
  0.0 25.3 jit_solution(9591908837766576658)
XLA Ops:
  0.0 23.4 %shard_map.91 = f32[256,512]{1,0:T(8,128)} custom-call(f32[256,512]{1,0:T(8,128)} %rhs_h.1, f32[1,256]{1,0:T(1,128)} %bitcast.1, f32[512,512]{1,0:T(8,128)} %st_h.1, f32[512,512]{1,0:T(8,128)} %li_h.1, f32[8,512]{1,0:T(8,128)} %modes_h.1, f32[8,256]{1,0:T(8,128)} %cw_h.1, s32[8,256]{1,0:T(8,128)} %cm_h.1, f32[8,256]{1,0:T(8,128)} %ci_h.1, s32[4,256]{1,0:T(4,128)} %nb_h.1), custom_call_target="tpu_custom_call" | custom-call | tf_op jit(solution)/shard_map/pallas_call | solution.py:392
  23.4 1.9 %copy.11 = f32[256,512]{1,0:T(8,128)} copy(f32[256,512]{1,0:T(8,128)} %shard_map.91) | data formatting | bytes 1048576

commit v4 on v3

--- a/solution.py
+++ b/solution.py
@@ -43,7 +43,7 @@
     rhs_h, kappa_h, st_h, li_h, modes_h, cw_h, cm_h, ci_h, nb_h,
     out_ref,
     rhs, kappa, st, li, modes, cw, cm, nb, cx,
-    msg, gbuf, hs, hbuf,
+    msg, merged, gbuf, sbuf, hs, hbuf,
     xh, xl, lh, ll, sh, sl, p_one, p_two, acc, w_one, z_one, pen,
     lsem, gsend, grecv, hsend, hrecv, csend, crecv,
 ):
@@ -70,28 +70,27 @@
 
     barrier = pltpu.get_barrier_semaphore()
 
-    peers = [lax.rem(grp + j, groups) for j in range(groups)]
-
-    def each_other(act):
-        def plane(i, carry):
-            other = lax.rem(sub + i, subs)
-            for peer in peers:
-                act((other, peer))
+    def each_in_group(act):
+        for i in range(1, groups):
+            act((sub, lax.rem(grp + i, groups)))
+
+    def each_in_stack(act):
+        def one(i, carry):
+            act((lax.rem(sub + i, subs), grp))
             return carry
 
         if subs <= 8:
             for i in sorted(range(1, subs), key=lambda i: abs(i - subs // 2)):
-                plane(i, 0)
+                one(i, 0)
         else:
-            lax.fori_loop(1, subs, plane, 0)
-        for peer in peers[1:]:
-            act((sub, peer))
-
-    each_other(
-        lambda target: pl.semaphore_signal(
-            barrier, inc=1, device_id=target, device_id_type=MESH
-        )
-    )
+            lax.fori_loop(1, subs, one, 0)
+
+    for each in (each_in_stack, each_in_group):
+        each(
+            lambda target: pl.semaphore_signal(
+                barrier, inc=1, device_id=target, device_id_type=MESH
+            )
+        )
     has_up, has_down = sub < subs - 1, sub > 0
 
     @pl.when(sub == 0)
@@ -104,23 +103,31 @@
         hbuf[:, BND:, :] = jnp.zeros((2, BND, LANES), F32)
         cx[2] = jnp.zeros(cx.shape[1:], F32)
 
-    def share(step):
-        each_other(
+    def send(step, stage, each, lines, place_of, slot):
+        each(
             lambda target: pltpu.make_async_remote_copy(
-                src_ref=msg.at[step],
-                dst_ref=gbuf.at[step, me],
-                send_sem=gsend.at[step],
-                recv_sem=grecv.at[step],
+                src_ref=lines.at[step],
+                dst_ref=place_of.at[step, slot],
+                send_sem=gsend.at[step, stage],
+                recv_sem=grecv.at[step, stage],
                 device_id=target,
                 device_id_type=MESH,
             ).start()
         )
-        gbuf[step, me] = msg[step]
-
-    def await_all(step, sem):
-        pltpu.make_async_copy(
-            gbuf.at[step, pl.ds(0, n - 1)], gbuf.at[step, pl.ds(0, n - 1)], sem.at[step]
-        ).wait()
+        place_of[step, slot] = lines[step]
+
+    def await_all(step, stage, sem):
+        place_of, count = (gbuf, groups) if stage == 0 else (sbuf, subs)
+        block = place_of.at[step, pl.ds(0, count - 1)]
+        pltpu.make_async_copy(block, block, sem.at[step, stage]).wait()
+
+    def share(step):
+        send(step, 0, each_in_group, msg, gbuf, grp)
+
+    def pass_on(step):
+        await_all(step, 0, grecv)
+        merged[step] = jnp.sum(gbuf[step], axis=0)
+        send(step, 1, each_in_stack, merged, sbuf, sub)
 
     lane = iota((1, LANES), 1)
     place = lax.rem(me, 16) * coarse
@@ -138,9 +145,10 @@
     def collect(step):
         chunks = []
         sums = jnp.zeros((1, LANES), F32)
+        per = 8 // groups
         for c in range(n // 16):
-            even = jnp.sum(gbuf[step, pl.ds(16 * c, 8)], axis=0)
-            odd = jnp.sum(gbuf[step, pl.ds(16 * c + 8, 8)], axis=0)
+            even = jnp.sum(sbuf[step, pl.ds(2 * per * c, per)], axis=0)
+            odd = jnp.sum(sbuf[step, pl.ds(2 * per * c + per, per)], axis=0)
             chunks.append(jnp.where(lane < HALF, even, odd))
             sums = sums + jnp.where(lane < HALF, odd, even)
         return chunks, sums
@@ -169,7 +177,7 @@
 
     split_to(rhs[...], xh, xl)
     fill(0, restrict(), [total(rhs[...] * rhs[...])])
-    pl.semaphore_wait(barrier, n - 1)
+    pl.semaphore_wait(barrier, groups + subs - 2)
     share(0)
 
     up = (lax.rem(sub + 1, subs), grp)
@@ -282,6 +290,7 @@
         acc[:, last:width] += jnp.where(first_half, 0.0, lifted)
 
     halo_one = start_local(0, p_one)
+    pass_on(0)
 
     loads[8].wait()
     split_to(st[...], sh, sl)
@@ -334,7 +343,7 @@
             spread, jnp.concatenate(values + [jnp.zeros_like(values[0])], axis=0).astype(BF16)
         )
 
-    await_all(0, grecv)
+    await_all(0, 1, grecv)
     chunks, sums = collect(0)
     beta = jnp.sqrt(scalar(sums, 0))
     scale = 1.0 / beta
@@ -349,10 +358,11 @@
     share(1)
 
     halo_two = start_local(1, p_two)
+    pass_on(1)
     finish_local(1, p_two, halo_two)
     z_one[...] = p_one[...] * scale + add_to_z(y)
 
-    await_all(1, grecv)
+    await_all(1, 1, grecv)
     chunks, sums = collect(1)
     h11 = scalar(sums, 0)
     s_one = scalar(sums, 1)
@@ -366,8 +376,9 @@
     fill(2, None, [first, second, third])
     share(2)
     p_two[...] = (p_two[...] + add_to_z(y) - h11 * z_one[...]) * over
-
-    await_all(2, grecv)
+    pass_on(2)
+
+    await_all(2, 1, grecv)
     chunks, sums = collect(2)
     h12, h22, s_two = scalar(sums, 0), scalar(sums, 1), scalar(sums, 2)
     cross = h11 * h12 + h21 * h22
@@ -377,14 +388,14 @@
     out_ref[...] = y_one * z_one[...] + y_two * p_two[...]
 
     for step in range(3):
-        await_all(step, gsend)
+        for stage in range(2):
+            await_all(step, stage, gsend)
     for copies in (coarse_copies, halo_one, halo_two):
         leave(copies)
 
 
 def body(subs, groups, rhs, kappa, stiffness, local_inverse, modes, cw, cm, ci, nb):
     rows, width = rhs.shape
-    n = subs * groups
     coarse, nc = ci.shape
     square = (width, width)
     vmem = pltpu.VMEM
@@ -398,13 +409,14 @@
             vmem((rows, width), F32), vmem((1, rows), F32), vmem(square, F32), vmem(square, F32),
             vmem((coarse, width), F32), vmem((coarse, rows), F32), vmem((coarse, rows), jnp.int32),
             vmem((4, rows), jnp.int32), vmem((3, coarse, nc + LANES), F32),
-            vmem((3, 1, LANES), F32), vmem((3, n, 1, LANES), F32),
+            vmem((3, 1, LANES), F32), vmem((3, 1, LANES), F32),
+            vmem((3, groups, 1, LANES), F32), vmem((3, subs, 1, LANES), F32),
             vmem((2, 2 * BND, LANES), F32), vmem((2, 2 * BND, LANES), F32),
             vmem((rows, width), BF16), vmem((rows, width), BF16),
             vmem(square, BF16), vmem(square, BF16), vmem(square, BF16), vmem(square, BF16),
             vmem((rows, width), F32), vmem((rows, width), F32), vmem((rows, width), F32),
             vmem((rows, width), F32), vmem((rows, width), F32), vmem((rows, LANES), F32),
-            dma((9,)), dma((3,)), dma((3,)), dma((2, 2)), dma((2, 2)), dma((2,)), dma((2,)),
+            dma((9,)), dma((3, 2)), dma((3, 2)), dma((2, 2)), dma((2, 2)), dma((2,)), dma((2,)),
         ],
         compiler_params=pltpu.CompilerParams(
             collective_id=0, has_side_effects=True, vmem_limit_bytes=int(62 * 1024 * 1024)

time: 25.5 us -> 29.3 us (1.15)
  Pallas kernels: 23.4 us -> 27.2 us
    pallas_call x1, Pallas kernels: 23.4 us -> 27.2 us  [body(): pl.pallas_call(functools.partial(kernel, subs, groups), out_shape=jax.Sha...]
where the time goes in v4:
time: 29.3 us; the launch traced here: 29.1 us
  Pallas kernels  27.2 us (93%)
  local copies, waits for them, and re-layouts  1.87 us (6%)
    pallas_call x1, Pallas kernels, body(): pl.pallas_call(functools.partial(kernel, subs, groups), out_shape=jax.Sha...  27.2 us
    unnamed x1, local copies, waits for them, and re-layouts  1.87 us

profile of v4, /device:TPU:0, one launch (start us, length us, event | category | flops | bytes accessed | tf_op | source)
XLA Modules:
  0.0 29.1 jit_solution(9093886765419267277)
XLA Ops:
  0.0 27.2 %shard_map.91 = f32[256,512]{1,0:T(8,128)} custom-call(f32[256,512]{1,0:T(8,128)} %rhs_h.1, f32[1,256]{1,0:T(1,128)} %bitcast.1, f32[512,512]{1,0:T(8,128)} %st_h.1, f32[512,512]{1,0:T(8,128)} %li_h.1, f32[8,512]{1,0:T(8,128)} %modes_h.1, f32[8,256]{1,0:T(8,128)} %cw_h.1, s32[8,256]{1,0:T(8,128)} %cm_h.1, f32[8,256]{1,0:T(8,128)} %ci_h.1, s32[4,256]{1,0:T(4,128)} %nb_h.1), custom_call_target="tpu_custom_call" | custom-call | tf_op jit(solution)/shard_map/pallas_call | solution.py:403
  27.2 1.9 %copy.11 = f32[256,512]{1,0:T(8,128)} copy(f32[256,512]{1,0:T(8,128)} %shard_map.91) | data formatting | bytes 1048576
